TPU v7x, 32 devices: a whole 2x2x4 slice. The times are simulated.
32 devices in a mesh: grp: 2 (over y), seq: 4 (over z), tp: 4 (over x, core).
Axes of the slice: x: 2, y: 2, z: 4, core: 2. Of those that a mesh axis runs over, the one named last changes fastest.
Arguments:
- grad_res: bfloat16 [4096, 4096], P(('grp', 'seq', 'tp')), parts along dimension 0, may hold values from -6 to 6
- features: bfloat16 [1536, 4608], P(('grp', 'seq', 'tp')), parts along dimension 0, may hold values from -70 to 70
- norm_gain: float32 [4608], replicated, may hold values from 0.1 to 1.9
- hidden_proj: bfloat16 [4608, 4608], P(None, 'tp'), may hold values from -0.09375 to 0.09375
- output_proj: bfloat16 [4608, 4096], P('tp'), may hold values from -0.09375 to 0.09375
- item_start: int32 [8, 32], P('grp'), parts along dimension 0, may hold values from 0 to 511, as said below
- item_len: int32 [8, 32], P('grp'), parts along dimension 0, may hold values from 3 to 6, as said below
- item_owner: int32 [8, 32], P('grp'), parts along dimension 0, may hold values from 0 to 3, as said below
Outputs:
- feat_grad: bfloat16 [1536, 4608], P(('grp', 'seq', 'tp')), parts along dimension 0
- grad_hidden: float32 [9216, 4608], P(('grp', 'seq'), 'tp'), parts along dimension 0
- grad_output: float32 [8192, 4608], P(('grp', 'seq'), 'tp'), parts along dimension 0
There are 2 independent parts, one for each index of `grp`. A program takes and returns all parts, laid end to end along the dimension named above; an argument that names none is the same for every part. Nothing has to cross between parts.
Inputs may be any that keep to these rules, and one draw needn't show every extreme that they name: `item_start`: items of a shard do not share tokens and stand in increasing order; item i lies within tokens t * 128 to (t + 1) * 128 - 1 of its shard, t = i // 8. `item_owner`: for each tp index t there is a permutation P_t of the owners such that item i of shard s goes to P_t[(s + i % 8) % 4], t = i // 8; so every owner gets exactly 8 items of each tp index. `item_len`: the items of one owner and one tp index hold at most 48 tokens, and the items of one device that go to one owner at most 12; in every draw one owner reaches both.
All inputs are finite; a program needn't handle non-finite values.
Results may differ from a plain program's by a relative error of at most 0.013.
Values may be sent and summed in bfloat16 or wider, within the bound.
A program may use at most 128 MiB of HBM per device.

v0:
```python
import jax
import jax.numpy as jnp
from jax import lax
from jax.sharding import PartitionSpec as P

EPSILON = 1e-06


def gelu_slope(pre_act):
    normal_cdf = 0.5 * (1.0 + lax.erf(pre_act * 0.7071067811865476))
    density = jnp.exp(-0.5 * pre_act * pre_act) * 0.3989422804014327
    return normal_cdf + pre_act * density


def outgoing_rows(grad_res, starts, lengths, owners, base_row, seq_count, slot_rows):
    item_count = owners.shape[0]
    order_index = jnp.arange(item_count)
    same_owner = owners[:, None] == owners[None, :]
    earlier = order_index[None, :] < order_index[:, None]
    offset = jnp.sum(jnp.where(same_owner & earlier, lengths[None, :], 0), axis=1)
    destination = jnp.arange(seq_count)[:, None, None]
    place_index = jnp.arange(slot_rows)[None, :, None]
    matched = (
        (owners[None, None, :] == destination)
        & (place_index >= offset)
        & (place_index < offset + lengths)
    )
    local_row = starts - base_row + place_index - offset
    source_row = jnp.sum(jnp.where(matched, local_row, 0), axis=2).reshape(-1)
    filled = jnp.any(matched, axis=2).reshape(-1, 1)
    picked = jnp.take(grad_res, source_row, axis=0)
    picked = jnp.where(filled, picked, jnp.zeros((), picked.dtype))
    return picked.reshape(seq_count, slot_rows, grad_res.shape[1])


def compact_rows(incoming, owner_table, length_table, seq_index, own_rows):
    seq_count, slot_rows, model_width = incoming.shape
    counts = jnp.sum(jnp.where(owner_table == seq_index, length_table, 0), axis=1)
    starts_at = jnp.cumsum(counts) - counts
    position = jnp.arange(own_rows)[:, None]
    inside = (position >= starts_at[None, :]) & (position < (starts_at + counts)[None, :])
    flat_index = jnp.arange(seq_count)[None, :] * slot_rows + position - starts_at[None, :]
    slot_index = jnp.sum(jnp.where(inside, flat_index, 0), axis=1)
    present = jnp.any(inside, axis=1)[:, None]
    gathered = jnp.take(incoming.reshape(seq_count * slot_rows, model_width), slot_index, axis=0)
    return jnp.where(present, gathered, jnp.zeros((), gathered.dtype))


def per_device(
    grad_res, features, norm_gain, hidden_proj, output_proj, item_start, item_len, item_owner
):
    seq_count = lax.axis_size("seq")
    lane_count = lax.axis_size("tp")
    seq_index = lax.axis_index("seq")
    lane_index = lax.axis_index("tp")
    tok_rows = grad_res.shape[0]
    own_rows = features.shape[0]
    item_count = item_len.shape[1] // lane_count
    longest = own_rows // item_count
    slot_rows = longest * max(1, item_count // seq_count)
    values = features.astype(jnp.float32)
    row_mean = jnp.mean(values, axis=1, keepdims=True)
    centered = values - row_mean
    variance = jnp.mean(centered * centered, axis=1, keepdims=True)
    inv_std = lax.rsqrt(variance + EPSILON)
    unit_rows = centered * inv_std
    normed_own = (unit_rows * norm_gain).astype(jnp.bfloat16)
    normed = lax.all_gather(normed_own, "tp", axis=0, tiled=True)
    first_item = lane_index * item_count
    starts = lax.dynamic_slice(item_start, (seq_index, first_item), (1, item_count))[0]
    lengths = lax.dynamic_slice(item_len, (seq_index, first_item), (1, item_count))[0]
    owners = lax.dynamic_slice(item_owner, (seq_index, first_item), (1, item_count))[0]
    outgoing = outgoing_rows(
        grad_res, starts, lengths, owners, lane_index * tok_rows, seq_count, slot_rows
    )
    incoming = lax.all_to_all(outgoing, "seq", split_axis=0, concat_axis=0, tiled=True)
    owner_table = lax.dynamic_slice_in_dim(item_owner, first_item, item_count, 1)
    length_table = lax.dynamic_slice_in_dim(item_len, first_item, item_count, 1)
    own_block = compact_rows(incoming, owner_table, length_table, seq_index, own_rows)
    routed = lax.all_gather(own_block, "tp", axis=0, tiled=True)
    pre_act = jnp.dot(normed, hidden_proj, preferred_element_type=jnp.float32)
    activated = jax.nn.gelu(pre_act, approximate=False).astype(jnp.bfloat16)
    grad_act = jnp.einsum("rd,hd->rh", routed, output_proj, preferred_element_type=jnp.float32)
    grad_pre = (grad_act * gelu_slope(pre_act)).astype(jnp.bfloat16)
    full_term = jnp.einsum("rh,mh->rm", grad_pre, hidden_proj, preferred_element_type=jnp.float32)
    summed = lax.psum(full_term.astype(jnp.bfloat16), "tp").astype(jnp.float32)
    own_grad = lax.dynamic_slice_in_dim(summed, lane_index * own_rows, own_rows, 0)
    scaled = own_grad * norm_gain
    grad_mean = jnp.mean(scaled, axis=1, keepdims=True)
    cross_mean = jnp.mean(scaled * unit_rows, axis=1, keepdims=True)
    feat_grad = ((scaled - grad_mean - unit_rows * cross_mean) * inv_std).astype(jnp.bfloat16)
    inverse = 1.0 / seq_count
    columns = normed
    grad_hidden = (
        lax.psum_scatter(
            jnp.einsum("rm,rh->mh", columns, grad_pre, preferred_element_type=jnp.float32).astype(
                jnp.bfloat16
            ),
            "seq",
            scatter_dimension=0,
            tiled=True,
        ).astype(jnp.float32)
        * inverse
    )
    columns = routed
    grad_output = (
        lax.psum_scatter(
            jnp.einsum("rd,rh->dh", columns, activated, preferred_element_type=jnp.float32).astype(
                jnp.bfloat16
            ),
            "seq",
            scatter_dimension=0,
            tiled=True,
        ).astype(jnp.float32)
        * inverse
    )
    return (feat_grad, grad_hidden, grad_output)


def solution(mesh):
    in_specs = (
        P(("grp", "seq", "tp"), None),
        P(("grp", "seq", "tp"), None),
        P(),
        P(None, "tp"),
        P("tp", None),
        P("grp", None),
        P("grp", None),
        P("grp", None),
    )
    out_specs = (P(("grp", "seq", "tp"), None), P(("grp", "seq"), "tp"), P(("grp", "seq"), "tp"))
    return jax.shard_map(
        per_device, mesh=mesh, in_specs=in_specs, out_specs=out_specs, check_vma=False
    )
```

profile of v0, /device:TPU:0, one launch (start us, length us, event | category | flops | bytes accessed | tf_op | source)
XLA Modules:
  0.0 478.2 jit_solution(12103437265287469871)
XLA Ops:
  7.2 0.0 all-gather.5.cloned.1.call-start
  7.2 1.2 convert_reduce_fusion
  8.5 1.3 fusion.11
  9.8 2.0 fusion.6
  11.8 0.0 all-gather.5.cloned.1.call-update
  11.8 0.8 dynamic-slice_bitcast_fusion.1
  12.6 0.8 subtract_bitcast_fusion
  13.4 0.2 select_reduce_fusion.1
  13.6 0.1 iota_compare_fusion.2
  13.6 0.1 add_subtract_fusion
  13.7 0.1 iota_compare_fusion
  13.8 0.1 select_reduce_fusion
  13.9 0.1 reshape.256
  14.0 0.1 fusion.58
  14.1 0.8 gather_fusion
  14.9 0.1 gather.11
  15.0 0.9 select_select_fusion
  15.9 6.3 %all-to-all-start = ((bf16[4,12,4096]{2,1,0:T(8,128)(2,1)}), bf16[4,12,4096]{2,1,0:T(8,128)(2,1)S(1)}, u32[]{:S(2)}, u32[]{:S(2)}) async-start(bf16[4,12,4096]{2,1,0:T(8,128)(2,1)} %select_select_fusion), calls=%async_computation | async-start | bytes 1048576 | tf_op jit(solution)/shard_map/all_to_all | solution.py:76
  22.3 0.2 select_reduce_fusion.3
  22.5 0.2 reduce-window.7
  22.6 0.1 select_reduce_fusion.2
  22.8 0.1 fusion.93
  22.9 13.9 %all-to-all-done = bf16[4,12,4096]{2,1,0:T(8,128)(2,1)S(1)} async-done(((bf16[4,12,4096]{2,1,0:T(8,128)(2,1)}), bf16[4,12,4096]{2,1,0:T(8,128)(2,1)S(1)}, u32[]{:S(2)}, u32[]{:S(2)}) %all-to-all-start) | async-done | bytes 393248 | tf_op jit(solution)/shard_map/all_to_all | solution.py:76
  36.7 0.1 reshape.257
  36.8 0.8 gather_fusion.1
  37.6 0.9 select_select_fusion.1
  38.5 0.0 all-gather.3.cloned.1.call-update
  38.5 0.0 all-reduce.2.cloned.1.call-start
  38.6 0.0 all-gather.5.cloned.1.call-done
  38.6 7.0 %fusion.94 = f32[192,1152]{1,0:T(8,128)S(1)} fusion(bf16[192,4608]{1,0:T(8,128)(2,1)} %all-gather.5.cloned.1.call-done, bf16[4608,1152]{1,0:T(8,128)(2,1)} %param.11), kind=kOutput, calls=%fused_computation.146 | convolution fusion | flops 2038431744 | bytes 13271040 | tf_op jit(solution)/shard_map/dot_general | solution.py:81
  45.6 11.8 %all-gather.3.cloned.1.call-done = bf16[192,4096]{1,0:T(8,128)(2,1)} async-done(((bf16[48,4096]{1,0:T(8,128)(2,1)}), bf16[192,4096]{1,0:T(8,128)(2,1)}) %all-gather.3.cloned.1.call-update) | async-done | bytes 1572880 | tf_op jit(solution)/shard_map/all_gather | solution.py:80
  57.5 7.5 %fusion = bf16[192,1152]{1,0:T(8,128)(2,1)S(1)} fusion(bf16[192,4096]{1,0:T(8,128)(2,1)} %all-gather.3.cloned.1.call-done, bf16[1152,4096]{1,0:T(8,128)(2,1)} %param.12, f32[192,1152]{1,0:T(8,128)S(1)} %fusion.94), kind=kOutput, calls=%fused_computation.8 | convolution fusion | flops 1814151168 | bytes 12337152 | tf_op jit(solution)/shard_map/rd,hd->rh/dot_general | solution.py:83
  65.0 9.0 %convolution_convert_fusion.2 = bf16[192,4608]{1,0:T(8,128)(2,1)} fusion(bf16[192,1152]{1,0:T(8,128)(2,1)S(1)} %fusion, bf16[4608,1152]{1,0:T(8,128)(2,1)} %param.11), kind=kOutput, calls=%fused_computation.4 | convolution fusion | flops 2039316480 | bytes 12828672 | tf_op jit(solution)/shard_map/rh,mh->rm/dot_general | solution.py:85
  74.0 0.0 all-reduce.2.cloned.1.call-update
  74.0 0.2 reduce-scatter.5.cloned.1.call-start
  74.2 8.9 %convolution_convert_fusion.1 = bf16[4096,1152]{1,0:T(8,128)(2,1)} fusion(bf16[192,4096]{1,0:T(8,128)(2,1)S(1)} %copy-done.7, f32[192,1152]{1,0:T(8,128)} %copy-done.8), kind=kOutput, calls=%fused_computation.3 | convolution fusion | flops 1831034880 | bytes 11894784 | tf_op jit(solution)/shard_map/rd,rh->dh/dot_general | solution.py:108
  83.1 0.0 reduce-scatter.5.cloned.1.call-update
  83.1 0.0 reduce-scatter.3.cloned.1.call-start
  83.2 1.4 copy-done.3
  84.6 5.9 %convolution_convert_fusion = bf16[4608,1152]{1,0:T(8,128)(2,1)} fusion(bf16[192,4608]{1,0:T(8,128)(2,1)S(1)} %copy-done.3, bf16[192,1152]{1,0:T(8,128)(2,1)S(1)} %fusion), kind=kOutput, calls=%fused_computation.2 | convolution fusion | flops 2043740160 | bytes 12828672 | tf_op jit(solution)/shard_map/rm,rh->mh/dot_general | solution.py:96
  90.5 0.0 reduce-scatter.3.cloned.1.call-update
  90.5 29.7 %all-reduce.2.cloned.1.call-done = bf16[192,4608]{1,0:T(8,128)(2,1)} async-done(((bf16[192,4608]{1,0:T(8,128)(2,1)}), bf16[192,4608]{1,0:T(8,128)(2,1)}) %all-reduce.2.cloned.1.call-update) | async-done | bytes 1769488 | tf_op jit(solution)/shard_map/psum | solution.py:86
  120.2 1.4 fusion.25
  121.6 2.1 fusion.10
  123.7 160.2 %reduce-scatter.5.cloned.1.call-done = bf16[1024,1152]{1,0:T(8,128)(2,1)} async-done(((bf16[4096,1152]{1,0:T(8,128)(2,1)}), bf16[1024,1152]{1,0:T(8,128)(2,1)}) %reduce-scatter.5.cloned.1.call-update) | async-done | bytes 2359312 | tf_op jit(solution)/shard_map/reduce_scatter | solution.py:107
  283.9 4.2 convert_multiply_fusion.1
  288.2 179.1 %reduce-scatter.3.cloned.1.call-done = bf16[1152,1152]{1,0:T(8,128)(2,1)} async-done(((bf16[4608,1152]{1,0:T(8,128)(2,1)}), bf16[1152,1152]{1,0:T(8,128)(2,1)}) %reduce-scatter.3.cloned.1.call-update) | async-done | bytes 2654224 | tf_op jit(solution)/shard_map/reduce_scatter | solution.py:95
  467.2 4.5 convert_multiply_fusion
  (32 shorter events, 0.1 us)
Async XLA Ops:
  7.2 6.9 %copy-start = (bf16[128,4096]{1,0:T(8,128)(2,1)S(1)}, bf16[128,4096]{1,0:T(8,128)(2,1)}, u32[]{:S(2)}) copy-start(bf16[128,4096]{1,0:T(8,128)(2,1)} %param.8) | copy-start | bytes 3145732
  7.2 15.1 %copy-start.6 = (s32[4,32]{1,0:T(4,128)S(1)}, s32[4,32]{1,0:T(4,128)}, u32[]{:S(2)}) copy-start(s32[4,32]{1,0:T(4,128)} %param.15) | copy-start | bytes 1540
  7.2 15.1 %copy-start.5 = (s32[4,32]{1,0:T(4,128)S(1)}, s32[4,32]{1,0:T(4,128)}, u32[]{:S(2)}) copy-start(s32[4,32]{1,0:T(4,128)} %param.14) | copy-start | bytes 1540
  7.2 31.4 %all-gather.5.cloned.1.call-start = ((), (), s32[]{:S(2)}) async-start(), calls=%async_computation.4 | async-start | bytes 2211840 | tf_op jit(solution)/shard_map/all_gather | solution.py:68
  15.9 20.8 %all-to-all-start = ((bf16[4,12,4096]{2,1,0:T(8,128)(2,1)}), bf16[4,12,4096]{2,1,0:T(8,128)(2,1)S(1)}, u32[]{:S(2)}, u32[]{:S(2)}) async-start(bf16[4,12,4096]{2,1,0:T(8,128)(2,1)} %select_select_fusion), calls=%async_computation | async-start | bytes 1048576 | tf_op jit(solution)/shard_map/all_to_all | solution.py:76
  22.3 35.2 %all-gather.3.cloned.1.call-start = ((), (), s32[]{:S(2)}) async-start(), calls=%async_computation.3 | async-start | bytes 1966080 | tf_op jit(solution)/shard_map/all_gather | solution.py:80
  38.5 81.7 %all-reduce.2.cloned.1.call-start = ((), (), s32[]{:S(2)}) async-start(), calls=%async_computation.5 | async-start | bytes 3538944 | tf_op jit(solution)/shard_map/psum | solution.py:86
  45.6 11.8 %copy-start.8 = (f32[192,1152]{1,0:T(8,128)}, f32[192,1152]{1,0:T(8,128)S(1)}, u32[]{:S(2)}) copy-start(f32[192,1152]{1,0:T(8,128)S(1)} %fusion.94) | copy-start | bytes 2654212
  65.0 9.3 %copy-start.7 = (bf16[192,4096]{1,0:T(8,128)(2,1)S(1)}, bf16[192,4096]{1,0:T(8,128)(2,1)}, u32[]{:S(2)}) copy-start(bf16[192,4096]{1,0:T(8,128)(2,1)} %all-gather.3.cloned.1.call-done) | copy-start | bytes 4718596
  74.0 209.9 %reduce-scatter.5.cloned.1.call-start = ((), (), s32[]{:S(2)}) async-start(), calls=%async_computation.7 | async-start | bytes 11796480 | tf_op jit(solution)/shard_map/reduce_scatter | solution.py:107
  83.1 1.5 copy-start.3
  83.1 384.1 %reduce-scatter.3.cloned.1.call-start = ((), (), s32[]{:S(2)}) async-start(), calls=%async_computation.6 | async-start | bytes 13271040 | tf_op jit(solution)/shard_map/reduce_scatter | solution.py:95
  90.5 29.7 %copy-start.2 = (bf16[48,4608]{1,0:T(8,128)(2,1)S(1)}, bf16[48,4608]{1,0:T(8,128)(2,1)}, u32[]{:S(2)}) copy-start(bf16[48,4608]{1,0:T(8,128)(2,1)} %param.9) | copy-start | bytes 1327108
  90.5 29.7 %copy-start.4 = (f32[4608]{0:T(1024)S(1)}, f32[4608]{0:T(1024)}, u32[]{:S(2)}) copy-start(f32[4608]{0:T(1024)} %param.10) | copy-start | bytes 55300
  283.9 187.8 %copy-start.1 = (bf16[128,4096]{1,0:T(8,128)(2,1)S(1)}, bf16[128,4096]{1,0:T(8,128)(2,1)}, u32[]{:S(2)}) copy-start(bf16[128,4096]{1,0:T(8,128)(2,1)} %param.8) | copy-start | bytes 3145732
Sparse Core Ops, SparseCore 0:
  12.0 23.4 all-gather.4
  38.7 18.7 all-gather.2
  74.1 46.0 all-reduce.1
  122.5 161.3 reduce-scatter.4
  286.2 180.9 reduce-scatter.2
where the time goes:
time: 479 us; the launch traced here: 478 us
  waiting for transfers between devices  395 us (82%)
  matrix products  38.3 us (8%)
  other arithmetic  20.5 us (4%)
  between operations  13.9 us (3%)
  starting transfers between devices  6.66 us (1%)
    reduce_scatter x1, waiting for transfers between devices, per_device(): lax.psum_scatter(jnp.einsum('rm,rh->mh', columns, grad_pre, preferred_ele...  179 us
    reduce_scatter x1, waiting for transfers between devices, per_device(): lax.psum_scatter(jnp.einsum('rd,rh->dh', columns, activated, preferred_el...  160 us
    psum x1, waiting for transfers between devices, per_device(): summed = lax.psum(full_term.astype(jnp.bfloat16), 'tp').astype(jnp.float32)  29.7 us
    all_to_all x1, waiting for transfers between devices, per_device(): lax.all_to_all(outgoing, 'seq', split_axis=0, concat_axis=0, tiled=True)  13.9 us
    all_gather x1, waiting for transfers between devices, per_device(): routed = lax.all_gather(own_block, 'tp', axis=0, tiled=True)  11.8 us
  transfers between devices with their start and end apart: 6, of which 5 were waited for; matrix products, arithmetic and copies ran while one was open for 8% of the time, Pallas kernels for 0%

commit v1 on v0

--- a/solution.py
+++ b/solution.py
@@ -117,7 +117,91 @@
     return (feat_grad, grad_hidden, grad_output)
 
 
+def pack_rows(grad_res, starts, lengths, base_row, own_rows):
+    item_count = lengths.shape[0]
+    longest = own_rows // item_count
+    step = jnp.arange(longest, dtype=jnp.int32)[None, :]
+    source = jnp.where(step < lengths[:, None], starts[:, None] - base_row + step, -1)
+    chosen = source.reshape(-1, 1) == jnp.arange(grad_res.shape[0], dtype=jnp.int32)[None, :]
+    return jnp.dot(
+        chosen.astype(jnp.bfloat16), grad_res, preferred_element_type=jnp.float32
+    ).astype(jnp.bfloat16)
+
+
+def destinations(item_len, item_owner, seq_count, lane_count, own_rows):
+    item_count = item_len.shape[1] // lane_count
+    longest = own_rows // item_count
+    shape = (seq_count, lane_count, item_count)
+    lengths = jnp.transpose(item_len.reshape(shape), (1, 0, 2)).reshape(lane_count, -1)
+    owners = jnp.transpose(item_owner.reshape(shape), (1, 0, 2)).reshape(lane_count, -1)
+    order = jnp.arange(seq_count * item_count)
+    before = (owners[:, :, None] == owners[:, None, :]) & (order[None, :] < order[:, None])
+    offset = jnp.sum(jnp.where(before, lengths[:, None, :], 0), axis=2)
+    first = (owners * lane_count + jnp.arange(lane_count)[:, None]) * own_rows + offset
+    step = jnp.arange(longest)
+    target = jnp.where(step < lengths[:, :, None], first[:, :, None] + step, -1)
+    target = target.reshape(lane_count, seq_count, item_count * longest)
+    return jnp.transpose(target, (1, 0, 2)).reshape(-1)
+
+
+def per_device_gathered(
+    grad_res, features, norm_gain, hidden_proj, output_proj, item_start, item_len, item_owner
+):
+    seq_count = lax.axis_size("seq")
+    lane_count = lax.axis_size("tp")
+    seq_index = lax.axis_index("seq")
+    lane_index = lax.axis_index("tp")
+    tok_rows = grad_res.shape[0]
+    own_rows = features.shape[0]
+    item_count = item_len.shape[1] // lane_count
+    owner_rows = own_rows * lane_count
+    values = features.astype(jnp.float32)
+    row_mean = jnp.mean(values, axis=1, keepdims=True)
+    centered = values - row_mean
+    variance = jnp.mean(centered * centered, axis=1, keepdims=True)
+    inv_std = lax.rsqrt(variance + EPSILON)
+    unit_rows = centered * inv_std
+    normed_own = (unit_rows * norm_gain).astype(jnp.bfloat16)
+    first_item = lane_index * item_count
+    starts = lax.dynamic_slice(item_start, (seq_index, first_item), (1, item_count))[0]
+    lengths = lax.dynamic_slice(item_len, (seq_index, first_item), (1, item_count))[0]
+    packed = pack_rows(grad_res, starts, lengths, lane_index * tok_rows, own_rows)
+    normed = lax.all_gather(normed_own, ("seq", "tp"), axis=0, tiled=True)
+    gathered = lax.all_gather(packed, ("seq", "tp"), axis=0, tiled=True)
+    target = destinations(item_len, item_owner, seq_count, lane_count, own_rows)
+    place = jnp.arange(target.shape[0])[:, None] == target[None, :]
+    routed = jnp.dot(
+        place.astype(jnp.bfloat16), gathered, preferred_element_type=jnp.float32
+    ).astype(jnp.bfloat16)
+    pre_act = jnp.dot(normed, hidden_proj, preferred_element_type=jnp.float32)
+    activated = jax.nn.gelu(pre_act, approximate=False).astype(jnp.bfloat16)
+    grad_act = jnp.einsum("rd,hd->rh", routed, output_proj, preferred_element_type=jnp.float32)
+    grad_pre = (grad_act * gelu_slope(pre_act)).astype(jnp.bfloat16)
+    own_pre = lax.dynamic_slice_in_dim(grad_pre, seq_index * owner_rows, owner_rows, 0)
+    full_term = jnp.einsum("rh,mh->rm", own_pre, hidden_proj, preferred_element_type=jnp.float32)
+    own_grad = lax.psum_scatter(
+        full_term.astype(jnp.bfloat16), "tp", scatter_dimension=0, tiled=True
+    ).astype(jnp.float32)
+    scaled = own_grad * norm_gain
+    grad_mean = jnp.mean(scaled, axis=1, keepdims=True)
+    cross_mean = jnp.mean(scaled * unit_rows, axis=1, keepdims=True)
+    feat_grad = ((scaled - grad_mean - unit_rows * cross_mean) * inv_std).astype(jnp.bfloat16)
+    inverse = 1.0 / seq_count
+    m_cut = normed.shape[1] // seq_count
+    d_cut = routed.shape[1] // seq_count
+    normed_cut = lax.dynamic_slice_in_dim(normed, seq_index * m_cut, m_cut, 1)
+    routed_cut = lax.dynamic_slice_in_dim(routed, seq_index * d_cut, d_cut, 1)
+    grad_hidden = (
+        jnp.einsum("rm,rh->mh", normed_cut, grad_pre, preferred_element_type=jnp.float32) * inverse
+    )
+    grad_output = (
+        jnp.einsum("rd,rh->dh", routed_cut, activated, preferred_element_type=jnp.float32) * inverse
+    )
+    return (feat_grad, grad_hidden, grad_output)
+
+
 def solution(mesh):
+    body = per_device_gathered if mesh.shape["seq"] <= 4 else per_device
     in_specs = (
         P(("grp", "seq", "tp"), None),
         P(("grp", "seq", "tp"), None),
@@ -130,5 +214,5 @@
     )
     out_specs = (P(("grp", "seq", "tp"), None), P(("grp", "seq"), "tp"), P(("grp", "seq"), "tp"))
     return jax.shard_map(
-        per_device, mesh=mesh, in_specs=in_specs, out_specs=out_specs, check_vma=False
-    )
+        body, mesh=mesh, in_specs=in_specs, out_specs=out_specs, check_vma=False
+    )

time: 479 us -> 219 us (0.46)
  waiting for transfers between devices: 395 us -> 128 us
  matrix products: 38.3 us -> 66.2 us
  other arithmetic: 20.5 us -> 9.06 us
  starting transfers between devices: 6.66 us -> 0.12 us
    reduce_scatter x2 -> x1, waiting for transfers between devices: 339 us -> 9.29 us  [per_device_gathered(): lax.psum_scatter(full_term.astype(jnp.bfloat16), 'tp', scatter_dimension=...]
    all_gather x2, waiting for transfers between devices: 11.8 us -> 119 us  [the longest x1 60.2 us: per_device_gathered(): gathered = lax.all_gather(packed, ('seq', 'tp'), axis=0, tiled=True)]
    psum x1 -> x0, waiting for transfers between devices: 29.7 us -> none  [per_device(): summed = lax.psum(full_term.astype(jnp.bfloat16), 'tp').astype(jnp.float32)]
    dot_general x5 -> x7, matrix products: 38.3 us -> 66.2 us  [the longest x1 17.2 us: per_device_gathered(): pre_act = jnp.dot(normed, hidden_proj, preferred_element_type=jnp.float32)]
    all_to_all x1 -> x0, waiting for transfers between devices: 13.9 us -> none  [per_device(): lax.all_to_all(outgoing, 'seq', split_axis=0, concat_axis=0, tiled=True)]
    mul x3 -> x0, other arithmetic: 8.72 us -> none  [the longest x1 4.47 us: per_device(): lax.psum_scatter(jnp.einsum('rm,rh->mh', columns, grad_pre, preferred_ele...]
    all_to_all x1 -> x0, starting transfers between devices: 6.32 us -> none  [per_device(): lax.all_to_all(outgoing, 'seq', split_axis=0, concat_axis=0, tiled=True)]
  transfers between devices with their start and end apart: 6 -> 3, of which waited for: 5 -> 3; matrix products, arithmetic and copies ran while one was open for 8% -> 16% of each run, Pallas kernels for 0% -> 0%
where the time goes in v1:
time: 219 us; the launch traced here: 218 us
  waiting for transfers between devices  128 us (58%)
  matrix products  66.2 us (30%)
  between operations  13.9 us (6%)
  other arithmetic  9.06 us (4%)
    all_gather x1, waiting for transfers between devices, per_device_gathered(): gathered = lax.all_gather(packed, ('seq', 'tp'), axis=0, tiled=True)  60.2 us
    all_gather x1, waiting for transfers between devices, per_device_gathered(): normed = lax.all_gather(normed_own, ('seq', 'tp'), axis=0, tiled=True)  58.4 us
    dot_general x1, matrix products, per_device_gathered(): pre_act = jnp.dot(normed, hidden_proj, preferred_element_type=jnp.float32)  17.2 us
    dot_general x1, matrix products, per_device_gathered(): jnp.einsum('rd,hd->rh', routed, output_proj, preferred_element_type=jnp.f...  14.6 us
    dot_general x1, matrix products, per_device_gathered(): jnp.einsum('rd,rh->dh', routed_cut, activated, preferred_element_type=jnp...  12.2 us
    dot_general x1, matrix products, per_device_gathered(): jnp.dot(place.astype(jnp.bfloat16), gathered, preferred_element_type=jnp....  9.75 us
    reduce_scatter x1, waiting for transfers between devices, per_device_gathered(): lax.psum_scatter(full_term.astype(jnp.bfloat16), 'tp', scatter_dimension=...  9.29 us
    dot_general x1, matrix products, per_device_gathered(): jnp.einsum('rm,rh->mh', normed_cut, grad_pre, preferred_element_type=jnp....  6.54 us
  transfers between devices with their start and end apart: 3, of which 3 were waited for; matrix products, arithmetic and copies ran while one was open for 16% of the time, Pallas kernels for 0%

profile of v1, /device:TPU:0, one launch (start us, length us, event | category | flops | bytes accessed | tf_op | source)
XLA Modules:
  0.0 218.3 jit_solution(16583443100387188197)
XLA Ops:
  7.2 0.0 copy-start
  7.2 0.0 copy-start.3
  7.2 0.0 copy-start.4
  7.2 0.0 all-gather.3.cloned.1.call-start
  7.3 0.8 subtract_bitcast_fusion
  8.1 0.1 add.94
  8.2 0.1 add.95
  8.3 0.1 lt.102
  8.3 0.1 lt.103
  8.4 0.1 lt.90
  8.5 0.0 copy-done
  8.5 1.1 convolution_convert_fusion.2
  9.6 0.0 all-gather.3.cloned.1.call-update
  9.6 0.0 all-gather.5.cloned.1.call-start
  9.7 1.2 convert_reduce_fusion
  10.9 1.3 fusion.59
  12.2 2.0 fusion.54
  14.2 0.0 all-gather.5.cloned.1.call-update
  14.2 0.0 reduce-scatter.2.cloned.1.call-start
  14.2 0.0 copy-done.3
  14.2 0.1 reshape.114
  14.3 0.0 copy-done.4
  14.3 0.1 reshape.115
  14.4 0.1 reshape.116
  14.5 0.1 lt.92
  14.6 0.2 select_reduce_fusion
  14.8 0.1 add.89
  14.9 0.1 add.90
  15.0 0.1 lt.93
  15.1 0.1 lt.94
  15.2 0.1 eq.45
  15.3 60.2 %all-gather.3.cloned.1.call-done = bf16[768,4096]{1,0:T(8,128)(2,1)} async-done(((bf16[48,4096]{1,0:T(8,128)(2,1)}), bf16[768,4096]{1,0:T(8,128)(2,1)}) %all-gather.3.cloned.1.call-update) | async-done | bytes 6291472 | tf_op jit(solution)/shard_map/all_gather | solution.py:170
  75.5 9.7 %convolution_convert_fusion = bf16[768,4096]{1,0:T(8,128)(2,1)} fusion(bf16[768,4096]{1,0:T(8,128)(2,1)} %all-gather.3.cloned.1.call-done, s32[768]{0:T(1024)S(1)} %eq.45), kind=kOutput, calls=%fused_computation.1 | convolution fusion | flops 4835573760 | bytes 12585984 | tf_op jit(solution)/shard_map/dot_general | solution.py:173
  85.2 58.4 %all-gather.5.cloned.1.call-done = bf16[768,4608]{1,0:T(8,128)(2,1)} async-done(((bf16[48,4608]{1,0:T(8,128)(2,1)}), bf16[768,4608]{1,0:T(8,128)(2,1)}) %all-gather.5.cloned.1.call-update) | async-done | bytes 7077904 | tf_op jit(solution)/shard_map/all_gather | solution.py:169
  143.6 17.2 %fusion.96 = f32[768,1152]{1,0:T(8,128)} fusion(bf16[768,4608]{1,0:T(8,128)(2,1)} %all-gather.5.cloned.1.call-done, bf16[4608,1152]{1,0:T(8,128)(2,1)} %param.11), kind=kOutput, calls=%fused_computation.127 | convolution fusion | flops 8153726976 | bytes 21233664 | tf_op jit(solution)/shard_map/dot_general | solution.py:176
  160.8 14.6 %fusion.14 = bf16[768,1152]{1,0:T(8,128)(2,1)S(1)} fusion(f32[768,1152]{1,0:T(8,128)} %fusion.96, bf16[768,4096]{1,0:T(8,128)(2,1)} %convolution_convert_fusion, bf16[1152,4096]{1,0:T(8,128)(2,1)} %param.12), kind=kOutput, calls=%fused_computation.30 | convolution fusion | flops 7256604672 | bytes 21037056 | tf_op jit(solution)/shard_map/rd,hd->rh/dot_general | solution.py:178
  175.4 0.0 slice-done
  175.4 0.0 slice-done.1
  175.4 0.0 slice-done.2
  175.4 4.9 %convolution_convert_fusion.1 = bf16[192,4608]{1,0:T(8,128)(2,1)} fusion(bf16[4608,1152]{1,0:T(8,128)(2,1)S(1)} %bitcast.19, bf16[768,1152]{1,0:T(8,128)(2,1)S(1)} %fusion.14, s32[]{:T(128)S(6)} %select_n.39), kind=kOutput, calls=%fused_computation.2 | convolution fusion | flops 2039316480 | bytes 12828676 | tf_op jit(solution)/shard_map/rh,mh->rm/dot_general | solution.py:181
  180.3 0.0 reduce-scatter.2.cloned.1.call-update
  180.3 0.0 copy-start.5
  180.3 6.5 %convolution_multiply_fusion = f32[1152,1152]{1,0:T(8,128)} fusion(bf16[768,1152]{1,0:T(8,128)(2,1)S(1)} %fusion.14, bf16[768,4608]{1,0:T(8,128)(2,1)} %all-gather.5.cloned.1.call-done, s32[]{:T(128)S(6)} %select_n.40), kind=kOutput, calls=%fused_computation | convolution fusion | flops 2039758848 | bytes 8847364 | tf_op jit(solution)/shard_map/rm,rh->mh/dot_general | solution.py:195
  186.9 12.2 %convolution_multiply_fusion.1 = f32[1024,1152]{1,0:T(8,128)} fusion(f32[768,1152]{1,0:T(8,128)S(1)} %copy-done.5, bf16[768,4096]{1,0:T(8,128)(2,1)} %convolution_convert_fusion, s32[]{:T(128)S(6)} %select_n.41), kind=kOutput, calls=%fused_computation.5 | convolution fusion | flops 1870626816 | bytes 9830404 | tf_op jit(solution)/shard_map/rd,rh->dh/dot_general | solution.py:198
  199.0 9.3 %reduce-scatter.2.cloned.1.call-done = bf16[48,4608]{1,0:T(8,128)(2,1)} async-done(((bf16[192,4608]{1,0:T(8,128)(2,1)}), bf16[48,4608]{1,0:T(8,128)(2,1)}) %reduce-scatter.2.cloned.1.call-update) | async-done | bytes 442384 | tf_op jit(solution)/shard_map/reduce_scatter | solution.py:182
  208.3 0.0 copy-done.1
  208.3 1.4 fusion.60
  209.7 2.1 fusion.58
  (20 shorter events, 0.1 us)
Async XLA Ops:
  7.2 1.3 copy-start
  7.2 7.0 %copy-start.3 = (s32[4,32]{1,0:T(4,128)S(1)}, s32[4,32]{1,0:T(4,128)}, u32[]{:S(2)}) copy-start(s32[4,32]{1,0:T(4,128)} %param.14) | copy-start | bytes 1540
  7.2 7.1 %copy-start.4 = (s32[4,32]{1,0:T(4,128)S(1)}, s32[4,32]{1,0:T(4,128)}, u32[]{:S(2)}) copy-start(s32[4,32]{1,0:T(4,128)} %param.15) | copy-start | bytes 1540
  7.2 68.3 %all-gather.3.cloned.1.call-start = ((), (), s32[]{:S(2)}) async-start(), calls=%async_computation.1 | async-start | bytes 6684672 | tf_op jit(solution)/shard_map/all_gather | solution.py:170
  9.6 134.0 %all-gather.5.cloned.1.call-start = ((), (), s32[]{:S(2)}) async-start(), calls=%async_computation.2 | async-start | bytes 7520256 | tf_op jit(solution)/shard_map/all_gather | solution.py:169
  14.2 194.1 %reduce-scatter.2.cloned.1.call-start = ((), (), s32[]{:S(2)}) async-start(), calls=%async_computation.3 | async-start | bytes 2211840 | tf_op jit(solution)/shard_map/reduce_scatter | solution.py:182
  143.6 31.8 %slice-start = ((s8[10616832]{0:T(1024)(128)(4,1)}), s8[4194304]{0:T(1024)(128)(4,1)S(1)}, s32[]{:S(2)}) async-start(s8[10616832]{0:T(1024)(128)(4,1)} %bitcast.18), calls=%async_computation.4 | async-start | bytes 8388608
  143.6 31.8 %slice-start.1 = ((s8[10616832]{0:T(1024)(128)(4,1)}), s8[4194304]{0:T(1024)(128)(4,1)S(1)}, s32[]{:S(2)}) async-start(s8[10616832]{0:T(1024)(128)(4,1)} %bitcast.18), calls=%async_computation.5 | async-start | bytes 8388608
  160.8 14.6 %slice-start.2 = ((s8[10616832]{0:T(1024)(128)(4,1)}), s8[2228224]{0:T(1024)(128)(4,1)S(1)}, s32[]{:S(2)}) async-start(s8[10616832]{0:T(1024)(128)(4,1)} %bitcast.18), calls=%async_computation.6 | async-start | bytes 4456448
  180.3 6.6 %copy-start.5 = (f32[768,1152]{1,0:T(8,128)S(1)}, f32[768,1152]{1,0:T(8,128)}, u32[]{:S(2)}) copy-start(f32[768,1152]{1,0:T(8,128)} %fusion.96) | copy-start | bytes 10616836
  186.9 21.5 %copy-start.1 = (bf16[48,4608]{1,0:T(8,128)(2,1)S(1)}, bf16[48,4608]{1,0:T(8,128)(2,1)}, u32[]{:S(2)}) copy-start(bf16[48,4608]{1,0:T(8,128)(2,1)} %param.9) | copy-start | bytes 1327108
  186.9 21.5 %copy-start.2 = (f32[4608]{0:T(1024)S(1)}, f32[4608]{0:T(1024)}, u32[]{:S(2)}) copy-start(f32[4608]{0:T(1024)} %param.10) | copy-start | bytes 55300
Sparse Core Ops, SparseCore 0:
  10.9 64.5 all-gather.2
  78.3 65.2 all-gather.4
  180.4 27.8 reduce-scatter.1

commit v2 on v1

--- a/solution.py
+++ b/solution.py
@@ -1,6 +1,8 @@
 import jax
 import jax.numpy as jnp
 from jax import lax
+from jax.experimental import pallas as pl
+from jax.experimental.pallas import tpu as pltpu
 from jax.sharding import PartitionSpec as P
 
 EPSILON = 1e-06
@@ -137,11 +139,354 @@
     order = jnp.arange(seq_count * item_count)
     before = (owners[:, :, None] == owners[:, None, :]) & (order[None, :] < order[:, None])
     offset = jnp.sum(jnp.where(before, lengths[:, None, :], 0), axis=2)
-    first = (owners * lane_count + jnp.arange(lane_count)[:, None]) * own_rows + offset
+    first = owners * own_rows + offset
     step = jnp.arange(longest)
     target = jnp.where(step < lengths[:, :, None], first[:, :, None] + step, -1)
-    target = target.reshape(lane_count, seq_count, item_count * longest)
-    return jnp.transpose(target, (1, 0, 2)).reshape(-1)
+    return target.reshape(lane_count, seq_count * item_count * longest)
+
+
+MESH = pl.DeviceIdType.MESH
+UP, DOWN, ACROSS, SIBLING, RELAY = range(5)
+
+
+def dot_nt(lhs, rhs):
+    return lax.dot_general(lhs, rhs, (((1,), (1,)), ((), ())), preferred_element_type=jnp.float32)
+
+
+def exchange_kernel(
+    normed_ref,
+    packed_ref,
+    place_ref,
+    hidden_hbm,
+    output_hbm,
+    grad_pre_ref,
+    active_ref,
+    normed_cut_ref,
+    routed_cut_ref,
+    own_grad_ref,
+    hidden_w,
+    output_w,
+    normed_all,
+    packed_all,
+    routed_all,
+    partial,
+    from_sibling,
+    to_across,
+    from_across,
+    load_sem,
+    send_sem,
+    recv_sem,
+    sum_send,
+    sum_recv,
+):
+    seq_count, lane_rows, m_width = normed_all.shape
+    rows = normed_ref.shape[0]
+    d_width = packed_ref.shape[1]
+    h_width = hidden_w.shape[1]
+    grp = lax.axis_index("grp")
+    me = lax.axis_index("seq")
+    lane = lax.axis_index("tp")
+    chip, core = lane // 2, lane % 2
+    sibling = chip * 2 + (1 - core)
+    across = (1 - chip) * 2 + core
+    diagonal = (1 - chip) * 2 + (1 - core)
+    last = seq_count - 1
+    has_up, has_down = me < last, me > 0
+
+    load_hidden = pltpu.make_async_copy(hidden_hbm, hidden_w, load_sem.at[0])
+    load_output = pltpu.make_async_copy(output_hbm, output_w, load_sem.at[1])
+    load_hidden.start()
+    load_output.start()
+
+    barrier = pltpu.get_barrier_semaphore()
+
+    def greet(seq_to, lane_to):
+        pl.semaphore_signal(
+            barrier, inc=1, device_id=(grp, seq_to, lane_to), device_id_type=MESH
+        )
+
+    greet(me, sibling)
+    greet(me, across)
+
+    @pl.when(has_up)
+    def _():
+        greet(me + 1, lane)
+
+    @pl.when(has_down)
+    def _():
+        greet(me - 1, lane)
+
+    pl.semaphore_wait(barrier, jnp.where((me == 0) | (me == last), 3, 4))
+
+    def slot(kind, plane, lane_at):
+        if kind == 0:
+            return normed_all.at[plane, pl.ds(pl.multiple_of(lane_at * rows, 16), rows)]
+        return packed_all.at[lane_at, pl.ds(pl.multiple_of(plane * rows, 16), rows)]
+
+    def copy(kind, plane, lane_at, way):
+        target = {
+            UP: (grp, jnp.minimum(me + 1, last), lane),
+            DOWN: (grp, jnp.maximum(me - 1, 0), lane),
+            ACROSS: (grp, me, across),
+            SIBLING: (grp, me, sibling),
+            RELAY: (grp, me, sibling),
+        }[way]
+        return pltpu.make_async_remote_copy(
+            src_ref=slot(kind, plane, lane_at),
+            dst_ref=slot(kind, plane, lane_at),
+            send_sem=send_sem.at[kind, way, plane],
+            recv_sem=recv_sem.at[kind, plane, lane_at],
+            device_id=target,
+            device_id_type=MESH,
+        )
+
+    def arrived(kind, plane, lane_at):
+        copy(kind, plane, lane_at, SIBLING).wait_recv()
+
+    mirrored = me >= seq_count // 2
+    near = jnp.where(mirrored, last - me, me)
+
+    def plane_at(step):
+        place = jnp.where((step < 2) & (near == 1), 1 - step, step)
+        return jnp.where(mirrored, last - place, place)
+
+    def along_seq(kind):
+        @pl.when(has_up)
+        def _():
+            copy(kind, me, lane, UP).start()
+
+        @pl.when(has_down)
+        def _():
+            copy(kind, me, lane, DOWN).start()
+
+    def own_out(kind):
+        copy(kind, me, lane, ACROSS).start()
+        copy(kind, me, lane, SIBLING).start()
+
+    def seq_stage(kind, step):
+        plane = plane_at(step)
+        arrived(kind, plane, lane)
+
+        @pl.when((plane < me) & has_up)
+        def _():
+            copy(kind, plane, lane, UP).start()
+
+        @pl.when((plane > me) & has_down)
+        def _():
+            copy(kind, plane, lane, DOWN).start()
+
+        copy(kind, plane, lane, ACROSS).start()
+        copy(kind, plane, lane, SIBLING).start()
+
+    def across_stage(kind, step):
+        plane = plane_at(step)
+        arrived(kind, plane, across)
+        copy(kind, plane, across, RELAY).start()
+
+    def sibling_stage(kind, step):
+        plane = plane_at(step)
+        arrived(kind, plane, sibling)
+        arrived(kind, plane, diagonal)
+
+    h_tile = h_width // 3
+
+    def activate(plane):
+        base = pl.multiple_of(plane * lane_rows, 16)
+
+        @pl.loop(0, 3)
+        def _(tile):
+            cols = pl.ds(pl.multiple_of(tile * h_tile, 128), h_tile)
+            pre_act = jnp.dot(
+                normed_all[plane], hidden_w[:, cols], preferred_element_type=jnp.float32
+            )
+            grad_act = dot_nt(routed_all[plane], output_w[cols, :])
+            normal_cdf = 0.5 * (1.0 + lax.erf(pre_act * 0.7071067811865476))
+            density = jnp.exp(-0.5 * pre_act * pre_act) * 0.3989422804014327
+            active_ref[pl.ds(base, lane_rows), cols] = (pre_act * normal_cdf).astype(jnp.bfloat16)
+            grad_pre_ref[pl.ds(base, lane_rows), cols] = (
+                grad_act * (normal_cdf + pre_act * density)
+            ).astype(jnp.bfloat16)
+
+    def place_rows():
+        width = d_width // 8
+
+        @pl.loop(0, 8)
+        def _(tile):
+            cols = pl.ds(pl.multiple_of(tile * width, 128), width)
+            for lane_at in range(place_ref.shape[0]):
+                placed = jnp.dot(
+                    place_ref[lane_at],
+                    packed_all[lane_at, :, cols],
+                    preferred_element_type=jnp.float32,
+                ).astype(jnp.bfloat16)
+                for owner in range(seq_count):
+                    routed_all[owner, lane_at * rows : (lane_at + 1) * rows, cols] = placed[
+                        owner * rows : (owner + 1) * rows
+                    ]
+
+    def partial_rows(lane_at):
+        return partial.at[pl.ds(pl.multiple_of(lane_at * rows, 16), rows)]
+
+    def sum_copy(index):
+        source, target, lane_to = (
+            (partial_rows(sibling), from_sibling.at[0], sibling),
+            (partial_rows(diagonal), from_sibling.at[1], sibling),
+            (to_across, from_across, across),
+        )[index]
+        return pltpu.make_async_remote_copy(
+            src_ref=source,
+            dst_ref=target,
+            send_sem=sum_send.at[index],
+            recv_sem=sum_recv.at[index],
+            device_id=(grp, me, lane_to),
+            device_id_type=MESH,
+        )
+
+    def own_partial():
+        own_pre = pl.ds(pl.multiple_of(me * lane_rows, 16), lane_rows)
+        width = m_width // 9
+
+        @pl.loop(0, 9)
+        def _(tile):
+            cols = pl.ds(pl.multiple_of(tile * width, 128), width)
+            partial[:, cols] = dot_nt(grad_pre_ref[own_pre, :], hidden_w[cols, :]).astype(
+                jnp.bfloat16
+            )
+
+    normed_all[me, pl.ds(pl.multiple_of(lane * rows, 16), rows), :] = normed_ref[...]
+    packed_all[lane, pl.ds(pl.multiple_of(me * rows, 16), rows), :] = packed_ref[...]
+
+    own_out(1)
+    along_seq(1)
+    own_out(0)
+    seq_stage(1, 1)
+    along_seq(0)
+    across_stage(1, 0)
+    across_stage(0, 0)
+    sibling_stage(1, 0)
+    sibling_stage(0, 0)
+    for step in range(2, seq_count):
+        seq_stage(1, step)
+        across_stage(1, step - 1)
+        sibling_stage(1, step - 1)
+    seq_stage(0, 1)
+    across_stage(1, last)
+    seq_stage(0, 2)
+    sibling_stage(1, last)
+    place_rows()
+    across_stage(0, 1)
+    load_hidden.wait()
+    load_output.wait()
+    activate(me)
+    own_partial()
+    sum_copy(0).start()
+    sum_copy(1).start()
+    seq_stage(0, 3)
+    across_stage(0, 2)
+    sibling_stage(0, 1)
+    activate(plane_at(1))
+    sum_copy(1).wait_recv()
+    to_across[...] = (
+        partial_rows(across)[...].astype(jnp.float32) + from_sibling[1].astype(jnp.float32)
+    ).astype(jnp.bfloat16)
+    sum_copy(2).start()
+    sibling_stage(0, 2)
+    activate(plane_at(2))
+    d_cut = routed_cut_ref.shape[1]
+    for owner in range(seq_count):
+        routed_cut_ref[owner * lane_rows : (owner + 1) * lane_rows, :] = routed_all[
+            owner, :, pl.ds(pl.multiple_of(me * d_cut, 128), d_cut)
+        ]
+    across_stage(0, 3)
+    sibling_stage(0, 3)
+    activate(plane_at(3))
+    m_cut = normed_cut_ref.shape[1]
+    for owner in range(seq_count):
+        normed_cut_ref[owner * lane_rows : (owner + 1) * lane_rows, :] = normed_all[
+            owner, :, pl.ds(pl.multiple_of(me * m_cut, 128), m_cut)
+        ]
+    sum_copy(0).wait_recv()
+    sum_copy(2).wait_recv()
+    own_grad_ref[...] = (
+        partial_rows(lane)[...].astype(jnp.float32)
+        + from_sibling[0].astype(jnp.float32)
+        + from_across[...].astype(jnp.float32)
+    )
+
+    for index in range(3):
+        sum_copy(index).wait_send()
+    for kind in (0, 1):
+        @pl.when(has_up)
+        def _():
+            copy(kind, me, lane, UP).wait_send()
+
+        @pl.when(has_down)
+        def _():
+            copy(kind, me, lane, DOWN).wait_send()
+
+        for step in range(seq_count):
+            plane = plane_at(step)
+            if step:
+                @pl.when((plane < me) & has_up)
+                def _():
+                    copy(kind, plane, lane, UP).wait_send()
+
+                @pl.when((plane > me) & has_down)
+                def _():
+                    copy(kind, plane, lane, DOWN).wait_send()
+
+            copy(kind, plane, lane, ACROSS).wait_send()
+            copy(kind, plane, lane, SIBLING).wait_send()
+            copy(kind, plane, across, RELAY).wait_send()
+
+
+def exchange(normed_own, packed, place, hidden_proj, output_proj, seq_count):
+    rows, m_width = normed_own.shape
+    d_width = packed.shape[1]
+    h_width = hidden_proj.shape[1]
+    lane_count = place.shape[0]
+    lane_rows = rows * lane_count
+    all_rows = lane_rows * seq_count
+    vmem = pl.BlockSpec(memory_space=pltpu.VMEM)
+    anywhere = pl.BlockSpec(memory_space=pl.ANY)
+    shape = jax.ShapeDtypeStruct
+    half = jnp.bfloat16
+    return pl.pallas_call(
+        exchange_kernel,
+        out_shape=(
+            shape((all_rows, h_width), half),
+            shape((all_rows, h_width), half),
+            shape((all_rows, m_width // seq_count), half),
+            shape((all_rows, d_width // seq_count), half),
+            shape((rows, m_width), jnp.float32),
+        ),
+        in_specs=[vmem, vmem, vmem, anywhere, anywhere],
+        out_specs=(vmem,) * 5,
+        scratch_shapes=[
+            pltpu.VMEM((m_width, h_width), half),
+            pltpu.VMEM((h_width, d_width), half),
+            pltpu.VMEM((seq_count, lane_rows, m_width), half),
+            pltpu.VMEM((lane_count, seq_count * rows, d_width), half),
+            pltpu.VMEM((seq_count, lane_rows, d_width), half),
+            pltpu.VMEM((lane_rows, m_width), half),
+            pltpu.VMEM((2, rows, m_width), half),
+            pltpu.VMEM((rows, m_width), half),
+            pltpu.VMEM((rows, m_width), half),
+            pltpu.SemaphoreType.DMA((2,)),
+            pltpu.SemaphoreType.DMA((2, 5, seq_count)),
+            pltpu.SemaphoreType.DMA((2, seq_count, lane_count)),
+            pltpu.SemaphoreType.DMA((3,)),
+            pltpu.SemaphoreType.DMA((3,)),
+        ],
+        compiler_params=pltpu.CompilerParams(
+            collective_id=0, has_side_effects=True, vmem_limit_bytes=60 * 1024 * 1024
+        ),
+        cost_estimate=pl.CostEstimate(
+            flops=2 * all_rows * h_width * (m_width + d_width),
+            bytes_accessed=2 * h_width * (m_width + d_width),
+            transcendentals=2 * all_rows * h_width,
+        ),
+    )(normed_own, packed, place, hidden_proj, output_proj)
 
 
 def per_device_gathered(
@@ -154,7 +499,6 @@
     tok_rows = grad_res.shape[0]
     own_rows = features.shape[0]
     item_count = item_len.shape[1] // lane_count
-    owner_rows = own_rows * lane_count
     values = features.astype(jnp.float32)
     row_mean = jnp.mean(values, axis=1, keepdims=True)
     centered = values - row_mean
@@ -166,31 +510,16 @@
     starts = lax.dynamic_slice(item_start, (seq_index, first_item), (1, item_count))[0]
     lengths = lax.dynamic_slice(item_len, (seq_index, first_item), (1, item_count))[0]
     packed = pack_rows(grad_res, starts, lengths, lane_index * tok_rows, own_rows)
-    normed = lax.all_gather(normed_own, ("seq", "tp"), axis=0, tiled=True)
-    gathered = lax.all_gather(packed, ("seq", "tp"), axis=0, tiled=True)
     target = destinations(item_len, item_owner, seq_count, lane_count, own_rows)
-    place = jnp.arange(target.shape[0])[:, None] == target[None, :]
-    routed = jnp.dot(
-        place.astype(jnp.bfloat16), gathered, preferred_element_type=jnp.float32
-    ).astype(jnp.bfloat16)
-    pre_act = jnp.dot(normed, hidden_proj, preferred_element_type=jnp.float32)
-    activated = jax.nn.gelu(pre_act, approximate=False).astype(jnp.bfloat16)
-    grad_act = jnp.einsum("rd,hd->rh", routed, output_proj, preferred_element_type=jnp.float32)
-    grad_pre = (grad_act * gelu_slope(pre_act)).astype(jnp.bfloat16)
-    own_pre = lax.dynamic_slice_in_dim(grad_pre, seq_index * owner_rows, owner_rows, 0)
-    full_term = jnp.einsum("rh,mh->rm", own_pre, hidden_proj, preferred_element_type=jnp.float32)
-    own_grad = lax.psum_scatter(
-        full_term.astype(jnp.bfloat16), "tp", scatter_dimension=0, tiled=True
-    ).astype(jnp.float32)
+    place = jnp.arange(seq_count * own_rows)[None, :, None] == target[:, None, :]
+    grad_pre, activated, normed_cut, routed_cut, own_grad = exchange(
+        normed_own, packed, place.astype(jnp.bfloat16), hidden_proj, output_proj, seq_count
+    )
     scaled = own_grad * norm_gain
     grad_mean = jnp.mean(scaled, axis=1, keepdims=True)
     cross_mean = jnp.mean(scaled * unit_rows, axis=1, keepdims=True)
     feat_grad = ((scaled - grad_mean - unit_rows * cross_mean) * inv_std).astype(jnp.bfloat16)
     inverse = 1.0 / seq_count
-    m_cut = normed.shape[1] // seq_count
-    d_cut = routed.shape[1] // seq_count
-    normed_cut = lax.dynamic_slice_in_dim(normed, seq_index * m_cut, m_cut, 1)
-    routed_cut = lax.dynamic_slice_in_dim(routed, seq_index * d_cut, d_cut, 1)
     grad_hidden = (
         jnp.einsum("rm,rh->mh", normed_cut, grad_pre, preferred_element_type=jnp.float32) * inverse
     )
@@ -201,7 +530,7 @@
 
 
 def solution(mesh):
-    body = per_device_gathered if mesh.shape["seq"] <= 4 else per_device
+    body = per_device_gathered if (mesh.shape["seq"], mesh.shape["tp"]) == (4, 4) else per_device
     in_specs = (
         P(("grp", "seq", "tp"), None),
         P(("grp", "seq", "tp"), None),

time: 219 us -> 130 us (0.59)
  waiting for transfers between devices: 128 us -> 0 us
  Pallas kernels: 0 us -> 105 us
  matrix products: 66.2 us -> 12.1 us
  between operations: 13.9 us -> 0.76 us
    all_gather x2 -> x0, waiting for transfers between devices: 119 us -> none  [the longest x1 60.2 us: per_device_gathered(): gathered = lax.all_gather(packed, ('seq', 'tp'), axis=0, tiled=True)]
    pallas_call x0 -> x1, Pallas kernels: none -> 105 us  [exchange(): pl.pallas_call(exchange_kernel, out_shape=(shape((all_rows, h_width), hal...]
    dot_general x4 -> x0, matrix products: 46.4 us -> none  [the longest x1 17.2 us: per_device_gathered(): pre_act = jnp.dot(normed, hidden_proj, preferred_element_type=jnp.float32)]
    reduce_scatter x1 -> x0, waiting for transfers between devices: 9.29 us -> none  [per_device_gathered(): lax.psum_scatter(full_term.astype(jnp.bfloat16), 'tp', scatter_dimension=...]
    dot_general x1, matrix products: 12.2 us -> 4.49 us  [per_device_gathered(): jnp.einsum('rd,rh->dh', routed_cut, activated, preferred_element_type=jnp...]
  transfers between devices with their start and end apart: 3 -> 0, of which waited for: 3 -> 0; matrix products, arithmetic and copies ran while one was open for 16% -> 0% of each run, Pallas kernels for 0% -> 0%
where the time goes in v2:
time: 130 us; the launch traced here: 129 us
  Pallas kernels  105 us (81%)
  matrix products  12.1 us (9%)
  other arithmetic  8.22 us (6%)
  local copies, waits for them, and re-layouts  2.32 us (2%)
    pallas_call x1, Pallas kernels, exchange(): pl.pallas_call(exchange_kernel, out_shape=(shape((all_rows, h_width), hal...  105 us
    dot_general x1, matrix products, per_device_gathered(): jnp.einsum('rm,rh->mh', normed_cut, grad_pre, preferred_element_type=jnp....  6.53 us
    dot_general x1, matrix products, per_device_gathered(): jnp.einsum('rd,rh->dh', routed_cut, activated, preferred_element_type=jnp...  4.49 us

profile of v2, /device:TPU:0, one launch (start us, length us, event | category | flops | bytes accessed | tf_op | source)
XLA Modules:
  0.0 128.6 jit_solution(5053493181776168145)
XLA Ops:
  0.6 0.0 copy-start
  0.6 0.0 copy-start.1
  0.7 0.0 copy-start.3
  0.7 0.9 subtract_bitcast_fusion
  1.6 1.2 convert_reduce_fusion
  2.7 1.3 %fusion.10 = f32[48]{0:T(128)S(1)} fusion(bf16[48,4608]{1,0:T(8,128)(2,1)} %param.9, f32[48]{0:T(128)S(1)} %broadcast_multiply_fusion.2), kind=kLoop, calls=%fused_computation.15 | loop fusion | flops 884688 | bytes 442752 | tf_op jit(solution)/shard_map/reduce_sum | solution.py:505
  4.1 0.1 add_select_fusion.1
  4.1 0.1 select_n.34
  4.2 0.8 reshape.132
  5.0 0.1 reshape.133
  5.1 0.8 reshape.131
  5.9 0.1 lt.88
  6.0 0.2 select_reduce_fusion
  6.2 0.1 lt.86
  6.3 0.1 add.66
  6.4 0.1 add.67
  6.5 0.1 lt.89
  6.6 0.1 lt.90
  6.7 0.9 fusion.11.place_ref
  7.6 0.0 copy-done
  7.6 1.1 convolution_convert_fusion.packed_ref
  8.6 0.0 copy-done.1
  8.6 0.0 copy-done.3
  8.6 1.0 fusion.5.normed_ref
  9.6 105.1 %shard_map.103 = (bf16[768,1152]{1,0:T(8,128)(2,1)}, bf16[768,1152]{1,0:T(8,128)(2,1)}, bf16[768,1152]{1,0:T(8,128)(2,1)}, bf16[768,1024]{1,0:T(8,128)(2,1)}, f32[48,4608]{1,0:T(8,128)}) custom-call(bf16[48,4608]{1,0:T(8,128)(2,1)} %fusion.5.normed_ref, bf16[48,4096]{1,0:T(8,128)(2,1)} %convolution_convert_fusion.packed_ref, ...), custom_call_target="tpu_custom_call" | custom-call | flops 15401484288 | bytes 20054016 | tf_op jit(solution)/shard_map/pallas_call | solution.py:454
  114.8 0.0 copy-start.2
  114.8 0.0 copy-start.6
  114.8 1.7 %multiply_reduce_fusion = (f32[48]{0:T(128)S(1)}, f32[48]{0:T(128)S(1)}) fusion(f32[48,4608]{1,0:T(8,128)} %get-tuple-element.8, f32[4608]{0:T(1024)S(1)} %copy-done.3, f32[48]{0:T(128)S(1)} %add_rsqrt_fusion, f32[48]{0:T(128)S(1)} %broadcast_multiply_fusion.2, bf16[48,4608]{1,0:T(8,128)(2,1)S(1)} %copy-done.1), kind=kLoop, calls=%fused_computation.18 | loop fusion | flops 1548192 | bytes 1346304 | tf_op jit(solution)/shard_map/reduce_sum | solution.py:519
  116.4 0.0 copy-done.2
  116.5 1.1 fusion.9
  117.5 0.0 copy-done.6
  117.5 0.0 copy-start.4
  117.5 0.0 copy-start.5
  117.5 6.5 %convolution_multiply_fusion = f32[1152,1152]{1,0:T(8,128)} fusion(bf16[768,1152]{1,0:T(8,128)(2,1)} %get-tuple-element.9, bf16[768,1152]{1,0:T(8,128)(2,1)S(1)} %copy-done.6), kind=kOutput, calls=%fused_computation | convolution fusion | flops 2039758848 | bytes 8847360 | tf_op jit(solution)/shard_map/rm,rh->mh/dot_general | solution.py:524
  124.1 0.0 copy-done.4
  124.1 0.0 copy-done.5
  124.1 4.5 %convolution_multiply_fusion.1 = f32[1024,1152]{1,0:T(8,128)} fusion(bf16[768,1024]{1,0:T(8,128)(2,1)S(1)} %copy-done.5, bf16[768,1152]{1,0:T(8,128)(2,1)S(1)} %copy-done.4), kind=kOutput, calls=%fused_computation.1 | convolution fusion | flops 1813118976 | bytes 8060928 | tf_op jit(solution)/shard_map/rd,rh->dh/dot_general | solution.py:527
  (10 shorter events, 0.1 us)
Async XLA Ops:
  0.6 6.9 %copy-start = (bf16[128,4096]{1,0:T(8,128)(2,1)S(1)}, bf16[128,4096]{1,0:T(8,128)(2,1)}, u32[]{:S(2)}) copy-start(bf16[128,4096]{1,0:T(8,128)(2,1)} %param.8) | copy-start | bytes 3145732
  0.6 8.0 %copy-start.1 = (bf16[48,4608]{1,0:T(8,128)(2,1)S(1)}, bf16[48,4608]{1,0:T(8,128)(2,1)}, u32[]{:S(2)}) copy-start(bf16[48,4608]{1,0:T(8,128)(2,1)} %param.9) | copy-start | bytes 1327108
  0.7 8.0 %copy-start.3 = (f32[4608]{0:T(1024)S(1)}, f32[4608]{0:T(1024)}, u32[]{:S(2)}) copy-start(f32[4608]{0:T(1024)} %param.10) | copy-start | bytes 55300
  114.8 1.7 %copy-start.2 = (f32[48,4608]{1,0:T(8,128)S(1)}, f32[48,4608]{1,0:T(8,128)}, u32[]{:S(2)}) copy-start(f32[48,4608]{1,0:T(8,128)} %get-tuple-element.8) | copy-start | bytes 2654212
  114.8 2.8 %copy-start.6 = (bf16[768,1152]{1,0:T(8,128)(2,1)S(1)}, bf16[768,1152]{1,0:T(8,128)(2,1)}, u32[]{:S(2)}) copy-start(bf16[768,1152]{1,0:T(8,128)(2,1)} %get-tuple-element.10) | copy-start | bytes 5308420
  117.5 6.5 %copy-start.4 = (bf16[768,1152]{1,0:T(8,128)(2,1)S(1)}, bf16[768,1152]{1,0:T(8,128)(2,1)}, u32[]{:S(2)}) copy-start(bf16[768,1152]{1,0:T(8,128)(2,1)} %get-tuple-element.12) | copy-start | bytes 5308420
  117.5 6.5 %copy-start.5 = (bf16[768,1024]{1,0:T(8,128)(2,1)S(1)}, bf16[768,1024]{1,0:T(8,128)(2,1)}, u32[]{:S(2)}) copy-start(bf16[768,1024]{1,0:T(8,128)(2,1)} %get-tuple-element.11) | copy-start | bytes 4718596

commit v3 on v2

--- a/solution.py
+++ b/solution.py
@@ -119,15 +119,13 @@
     return (feat_grad, grad_hidden, grad_output)
 
 
-def pack_rows(grad_res, starts, lengths, base_row, own_rows):
+def chosen_rows(starts, lengths, base_row, tok_rows, own_rows):
     item_count = lengths.shape[0]
     longest = own_rows // item_count
     step = jnp.arange(longest, dtype=jnp.int32)[None, :]
     source = jnp.where(step < lengths[:, None], starts[:, None] - base_row + step, -1)
-    chosen = source.reshape(-1, 1) == jnp.arange(grad_res.shape[0], dtype=jnp.int32)[None, :]
-    return jnp.dot(
-        chosen.astype(jnp.bfloat16), grad_res, preferred_element_type=jnp.float32
-    ).astype(jnp.bfloat16)
+    chosen = source.reshape(-1, 1) == jnp.arange(tok_rows, dtype=jnp.int32)[None, :]
+    return chosen.astype(jnp.bfloat16)
 
 
 def destinations(item_len, item_owner, seq_count, lane_count, own_rows):
@@ -146,7 +144,7 @@
 
 
 MESH = pl.DeviceIdType.MESH
-UP, DOWN, ACROSS, SIBLING, RELAY = range(5)
+UP, DOWN, ACROSS, SIBLING, RELAY, PAIR = range(6)
 
 
 def dot_nt(lhs, rhs):
@@ -154,8 +152,10 @@
 
 
 def exchange_kernel(
-    normed_ref,
-    packed_ref,
+    features_ref,
+    gain_ref,
+    chosen_ref,
+    grad_res_ref,
     place_ref,
     hidden_hbm,
     output_hbm,
@@ -163,7 +163,7 @@
     active_ref,
     normed_cut_ref,
     routed_cut_ref,
-    own_grad_ref,
+    feat_grad_ref,
     hidden_w,
     output_w,
     normed_all,
@@ -180,8 +180,8 @@
     sum_recv,
 ):
     seq_count, lane_rows, m_width = normed_all.shape
-    rows = normed_ref.shape[0]
-    d_width = packed_ref.shape[1]
+    rows = features_ref.shape[0]
+    d_width = grad_res_ref.shape[1]
     h_width = hidden_w.shape[1]
     grp = lax.axis_index("grp")
     me = lax.axis_index("seq")
@@ -216,6 +216,15 @@
     def _():
         greet(me - 1, lane)
 
+    pack_width = d_width // 8
+
+    @pl.loop(0, 8)
+    def _(tile):
+        cols = pl.ds(pl.multiple_of(tile * pack_width, 128), pack_width)
+        packed_all[lane, pl.ds(pl.multiple_of(me * rows, 16), rows), cols] = jnp.dot(
+            chosen_ref[...], grad_res_ref[:, cols], preferred_element_type=jnp.float32
+        ).astype(jnp.bfloat16)
+
     pl.semaphore_wait(barrier, jnp.where((me == 0) | (me == last), 3, 4))
 
     def slot(kind, plane, lane_at):
@@ -230,6 +239,7 @@
             ACROSS: (grp, me, across),
             SIBLING: (grp, me, sibling),
             RELAY: (grp, me, sibling),
+            PAIR: (grp, pair, lane),
         }[way]
         return pltpu.make_async_remote_copy(
             src_ref=slot(kind, plane, lane_at),
@@ -250,6 +260,18 @@
         place = jnp.where((step < 2) & (near == 1), 1 - step, step)
         return jnp.where(mirrored, last - place, place)
 
+    pair = me + 1 - 2 * (me % 2)
+    at_end = (me == 0) | (me == last)
+
+    def when_spared(act):
+        pl.when(at_end)(act)
+
+    def when_crossed(step, act):
+        if step != 1:
+            act()
+        else:
+            pl.when(at_end)(act)
+
     def along_seq(kind):
         @pl.when(has_up)
         def _():
@@ -275,12 +297,14 @@
         def _():
             copy(kind, plane, lane, DOWN).start()
 
-        copy(kind, plane, lane, ACROSS).start()
+        when_crossed(step, lambda: copy(kind, plane, lane, ACROSS).start())
         copy(kind, plane, lane, SIBLING).start()
 
     def across_stage(kind, step):
         plane = plane_at(step)
         arrived(kind, plane, across)
+        if step == 0:
+            when_spared(lambda: copy(kind, me, across, PAIR).start())
         copy(kind, plane, across, RELAY).start()
 
     def sibling_stage(kind, step):
@@ -353,26 +377,41 @@
                 jnp.bfloat16
             )
 
-    normed_all[me, pl.ds(pl.multiple_of(lane * rows, 16), rows), :] = normed_ref[...]
-    packed_all[lane, pl.ds(pl.multiple_of(me * rows, 16), rows), :] = packed_ref[...]
+    def unit_and_scale():
+        values = features_ref[...].astype(jnp.float32)
+        centered = values - jnp.mean(values, axis=1, keepdims=True)
+        variance = jnp.mean(centered * centered, axis=1, keepdims=True)
+        inv_std = lax.rsqrt(variance + EPSILON)
+        return centered * inv_std, inv_std
 
     own_out(1)
     along_seq(1)
+    unit_rows, inv_std = unit_and_scale()
+    normed_all[me, pl.ds(pl.multiple_of(lane * rows, 16), rows), :] = (
+        unit_rows * gain_ref[...]
+    ).astype(jnp.bfloat16)
     own_out(0)
     seq_stage(1, 1)
     along_seq(0)
     across_stage(1, 0)
+    seq_stage(1, 2)
+    seq_stage(1, 3)
     across_stage(0, 0)
+    across_stage(1, 1)
+    seq_stage(0, 1)
     sibling_stage(1, 0)
     sibling_stage(0, 0)
-    for step in range(2, seq_count):
-        seq_stage(1, step)
-        across_stage(1, step - 1)
-        sibling_stage(1, step - 1)
-    seq_stage(0, 1)
-    across_stage(1, last)
+    across_stage(1, 2)
+    sibling_stage(1, 1)
     seq_stage(0, 2)
-    sibling_stage(1, last)
+    across_stage(1, 3)
+
+    @pl.when(jnp.logical_not(at_end))
+    def _():
+        seq_stage(0, 3)
+
+    sibling_stage(1, 2)
+    sibling_stage(1, 3)
     place_rows()
     across_stage(0, 1)
     load_hidden.wait()
@@ -381,7 +420,11 @@
     own_partial()
     sum_copy(0).start()
     sum_copy(1).start()
-    seq_stage(0, 3)
+
+    @pl.when(at_end)
+    def _():
+        seq_stage(0, 3)
+
     across_stage(0, 2)
     sibling_stage(0, 1)
     activate(plane_at(1))
@@ -407,15 +450,24 @@
         ]
     sum_copy(0).wait_recv()
     sum_copy(2).wait_recv()
-    own_grad_ref[...] = (
+    own_grad = (
         partial_rows(lane)[...].astype(jnp.float32)
         + from_sibling[0].astype(jnp.float32)
         + from_across[...].astype(jnp.float32)
     )
+    unit_rows, inv_std = unit_and_scale()
+    scaled = own_grad * gain_ref[...]
+    grad_mean = jnp.mean(scaled, axis=1, keepdims=True)
+    cross_mean = jnp.mean(scaled * unit_rows, axis=1, keepdims=True)
+    feat_grad_ref[...] = ((scaled - grad_mean - unit_rows * cross_mean) * inv_std).astype(
+        jnp.bfloat16
+    )
 
     for index in range(3):
         sum_copy(index).wait_send()
     for kind in (0, 1):
+        when_spared(lambda: copy(kind, me, across, PAIR).wait_send())
+
         @pl.when(has_up)
         def _():
             copy(kind, me, lane, UP).wait_send()
@@ -435,14 +487,14 @@
                 def _():
                     copy(kind, plane, lane, DOWN).wait_send()
 
-            copy(kind, plane, lane, ACROSS).wait_send()
+            when_crossed(step, lambda: copy(kind, plane, lane, ACROSS).wait_send())
             copy(kind, plane, lane, SIBLING).wait_send()
             copy(kind, plane, across, RELAY).wait_send()
 
 
-def exchange(normed_own, packed, place, hidden_proj, output_proj, seq_count):
-    rows, m_width = normed_own.shape
-    d_width = packed.shape[1]
+def exchange(features, norm_gain, chosen, grad_res, place, hidden_proj, output_proj, seq_count):
+    rows, m_width = features.shape
+    d_width = grad_res.shape[1]
     h_width = hidden_proj.shape[1]
     lane_count = place.shape[0]
     lane_rows = rows * lane_count
@@ -458,9 +510,9 @@
             shape((all_rows, h_width), half),
             shape((all_rows, m_width // seq_count), half),
             shape((all_rows, d_width // seq_count), half),
-            shape((rows, m_width), jnp.float32),
+            shape((rows, m_width), half),
         ),
-        in_specs=[vmem, vmem, vmem, anywhere, anywhere],
+        in_specs=[vmem, vmem, vmem, vmem, vmem, anywhere, anywhere],
         out_specs=(vmem,) * 5,
         scratch_shapes=[
             pltpu.VMEM((m_width, h_width), half),
@@ -473,7 +525,7 @@
             pltpu.VMEM((rows, m_width), half),
             pltpu.VMEM((rows, m_width), half),
             pltpu.SemaphoreType.DMA((2,)),
-            pltpu.SemaphoreType.DMA((2, 5, seq_count)),
+            pltpu.SemaphoreType.DMA((2, 6, seq_count)),
             pltpu.SemaphoreType.DMA((2, seq_count, lane_count)),
             pltpu.SemaphoreType.DMA((3,)),
             pltpu.SemaphoreType.DMA((3,)),
@@ -486,7 +538,7 @@
             bytes_accessed=2 * h_width * (m_width + d_width),
             transcendentals=2 * all_rows * h_width,
         ),
-    )(normed_own, packed, place, hidden_proj, output_proj)
+    )(features, norm_gain.reshape(1, m_width), chosen, grad_res, place, hidden_proj, output_proj)
 
 
 def per_device_gathered(
@@ -499,26 +551,22 @@
     tok_rows = grad_res.shape[0]
     own_rows = features.shape[0]
     item_count = item_len.shape[1] // lane_count
-    values = features.astype(jnp.float32)
-    row_mean = jnp.mean(values, axis=1, keepdims=True)
-    centered = values - row_mean
-    variance = jnp.mean(centered * centered, axis=1, keepdims=True)
-    inv_std = lax.rsqrt(variance + EPSILON)
-    unit_rows = centered * inv_std
-    normed_own = (unit_rows * norm_gain).astype(jnp.bfloat16)
     first_item = lane_index * item_count
     starts = lax.dynamic_slice(item_start, (seq_index, first_item), (1, item_count))[0]
     lengths = lax.dynamic_slice(item_len, (seq_index, first_item), (1, item_count))[0]
-    packed = pack_rows(grad_res, starts, lengths, lane_index * tok_rows, own_rows)
+    chosen = chosen_rows(starts, lengths, lane_index * tok_rows, tok_rows, own_rows)
     target = destinations(item_len, item_owner, seq_count, lane_count, own_rows)
     place = jnp.arange(seq_count * own_rows)[None, :, None] == target[:, None, :]
-    grad_pre, activated, normed_cut, routed_cut, own_grad = exchange(
-        normed_own, packed, place.astype(jnp.bfloat16), hidden_proj, output_proj, seq_count
-    )
-    scaled = own_grad * norm_gain
-    grad_mean = jnp.mean(scaled, axis=1, keepdims=True)
-    cross_mean = jnp.mean(scaled * unit_rows, axis=1, keepdims=True)
-    feat_grad = ((scaled - grad_mean - unit_rows * cross_mean) * inv_std).astype(jnp.bfloat16)
+    grad_pre, activated, normed_cut, routed_cut, feat_grad = exchange(
+        features,
+        norm_gain,
+        chosen,
+        grad_res,
+        place.astype(jnp.bfloat16),
+        hidden_proj,
+        output_proj,
+        seq_count,
+    )
     inverse = 1.0 / seq_count
     grad_hidden = (
         jnp.einsum("rm,rh->mh", normed_cut, grad_pre, preferred_element_type=jnp.float32) * inverse

time: 130 us -> 121 us (0.931)
  other arithmetic: 8.22 us -> 2.62 us
  Pallas kernels: 105 us -> 100 us
  local copies, waits for them, and re-layouts: 2.32 us -> 4.4 us
    pallas_call x1, Pallas kernels: 105 us -> 100 us  [exchange(): pl.pallas_call(exchange_kernel, out_shape=(shape((all_rows, h_width), hal...]
    reduce_sum x3 -> x0, other arithmetic: 4.13 us -> none  [the longest x1 1.65 us: per_device_gathered(): grad_mean = jnp.mean(scaled, axis=1, keepdims=True)]
    reshape x0 -> x1, local copies, waits for them, and re-layouts: none -> 1.35 us  [exchange(): norm_gain.reshape(1, m_width)]
    convert_element_type x2 -> x1, other arithmetic: 2.02 us -> 0.68 us  [chosen_rows(): return chosen.astype(jnp.bfloat16)]
where the time goes in v3:
time: 121 us; the launch traced here: 120 us
  Pallas kernels  100 us (83%)
  matrix products  11.5 us (10%)
  local copies, waits for them, and re-layouts  4.4 us (4%)
  other arithmetic  2.62 us (2%)
    pallas_call x1, Pallas kernels, exchange(): pl.pallas_call(exchange_kernel, out_shape=(shape((all_rows, h_width), hal...  100 us
    dot_general x1, matrix products, per_device_gathered(): jnp.einsum('rm,rh->mh', normed_cut, grad_pre, preferred_element_type=jnp....  7.04 us
    dot_general x1, matrix products, per_device_gathered(): jnp.einsum('rd,rh->dh', routed_cut, activated, preferred_element_type=jnp...  4.49 us

profile of v3, /device:TPU:0, one launch (start us, length us, event | category | flops | bytes accessed | tf_op | source)
XLA Modules:
  0.0 119.6 jit_solution(17621374627165882290)
XLA Ops:
  0.6 1.3 %reshape.113.gain_ref = f32[1,4608]{1,0:T(1,128)} reshape(f32[4608]{0:T(1024)} %param.10) | data formatting | bytes 36864 | tf_op jit(solution)/shard_map/reshape | solution.py:541
  2.0 0.8 subtract_bitcast_fusion
  2.7 0.1 add_select_fusion.1
  2.8 0.1 select_n.34
  2.9 0.7 fusion.1.chosen_ref
  3.6 0.8 reshape.114
  4.4 0.1 lt.88
  4.4 0.8 reshape.115
  5.2 0.1 reshape.116
  5.3 0.2 select_reduce_fusion
  5.5 0.1 add.53
  5.6 0.1 add.54
  5.7 0.1 lt.89
  5.8 0.1 lt.90
  5.9 0.1 lt.86
  6.1 0.9 fusion.place_ref
  6.9 100.4 %shard_map.103 = (bf16[768,1152]{1,0:T(8,128)(2,1)}, bf16[768,1152]{1,0:T(8,128)(2,1)}, bf16[768,1152]{1,0:T(8,128)(2,1)}, bf16[768,1024]{1,0:T(8,128)(2,1)}, bf16[48,4608]{1,0:T(8,128)(2,1)}) custom-call(bf16[48,4608]{1,0:T(8,128)(2,1)} %features_ref.1, f32[1,4608]{1,0:T(1,128)} %reshape.113.gain_ref, bf16[48,128]{1,0:T(8,128)(2,1)} %fusion.1.chosen_ref, ...), custom_call_target="tpu_custom_call" | custom-call | flops 15401484288 | bytes 20054016 | tf_op jit(solution)/shard_map/pallas_call | solution.py:506
  107.3 0.0 copy-start.1
  107.3 0.0 copy-start.2
  107.3 7.0 %convolution_multiply_fusion = f32[1152,1152]{1,0:T(8,128)} fusion(bf16[768,1152]{1,0:T(8,128)(2,1)} %get-tuple-element.9, bf16[768,1152]{1,0:T(8,128)(2,1)} %get-tuple-element.10), kind=kOutput, calls=%fused_computation | convolution fusion | flops 2039758848 | bytes 8847360 | tf_op jit(solution)/shard_map/rm,rh->mh/dot_general | solution.py:572
  114.4 0.0 copy-done.1
  114.4 0.0 copy-done.2
  114.4 0.0 copy-start
  114.4 4.5 %convolution_multiply_fusion.1 = f32[1024,1152]{1,0:T(8,128)} fusion(bf16[768,1024]{1,0:T(8,128)(2,1)S(1)} %copy-done.2, bf16[768,1152]{1,0:T(8,128)(2,1)S(1)} %copy-done.1), kind=kOutput, calls=%fused_computation.1 | convolution fusion | flops 1813118976 | bytes 8060928 | tf_op jit(solution)/shard_map/rd,rh->dh/dot_general | solution.py:575
  118.9 0.0 copy-done
  118.9 0.8 copy.18
  (6 shorter events, 0.0 us)
Async XLA Ops:
  107.3 7.1 %copy-start.1 = (bf16[768,1152]{1,0:T(8,128)(2,1)S(1)}, bf16[768,1152]{1,0:T(8,128)(2,1)}, u32[]{:S(2)}) copy-start(bf16[768,1152]{1,0:T(8,128)(2,1)} %get-tuple-element.12) | copy-start | bytes 5308420
  107.3 7.1 %copy-start.2 = (bf16[768,1024]{1,0:T(8,128)(2,1)S(1)}, bf16[768,1024]{1,0:T(8,128)(2,1)}, u32[]{:S(2)}) copy-start(bf16[768,1024]{1,0:T(8,128)(2,1)} %get-tuple-element.11) | copy-start | bytes 4718596
  114.4 4.5 %copy-start = (bf16[48,4608]{1,0:T(8,128)(2,1)S(1)}, bf16[48,4608]{1,0:T(8,128)(2,1)}, u32[]{:S(2)}) copy-start(bf16[48,4608]{1,0:T(8,128)(2,1)} %get-tuple-element.18) | copy-start | bytes 1327108
